TPU v7x, 512 devices: a whole 4x4x16 slice. The times are simulated.
512 devices in a mesh: enc: 16 (over x, z_hi), seq: 8 (over y, core), tp: 4 (over z_lo).
Axes of the slice: x: 4, y: 4, z: 16 (z_hi: 4, z_lo: 4; z = z_hi * 4 + z_lo), core: 2. Of those that a mesh axis runs over, the one named last changes fastest.
Arguments:
- visual_key_value: bfloat16 [16, 16, 256, 2048], P(None, 'seq', 'enc', 'tp'), may hold values from -4.5 to 4.5
- patch_blocks: int32 [16, 16], P('enc'), may hold values from 1 to 8
- queries: bfloat16 [16, 16, 32, 8192], P('enc', 'seq', None, 'tp'), may hold values from -113 to 113
- suffix_key_value: bfloat16 [16, 16, 32, 2048], P('enc', 'seq', None, 'tp'), may hold values from -6 to 6
- suffix_hidden_state: bfloat16 [16, 16, 32, 8192], P('enc', 'seq', None, 'tp'), may hold values from -6 to 6
- down_weight: bfloat16 [8192, 128], P('tp'), may hold values from -0.0625 to 0.0625
- up_weight: bfloat16 [128, 8192], P(None, 'tp'), may hold values from -1.5 to 1.5
- question_adapter: int32 [16, 16], P('enc', 'seq'), may hold values from 0 to 7
- suffix_token_length: int32 [16, 16], P('enc', 'seq'), may hold values from 1 to 32
Outputs:
- context: bfloat16 [16, 16, 32, 8192], P('enc', 'seq', None, 'tp')
All inputs are finite; a program needn't handle non-finite values.
Results may differ from a plain program's by a relative error of at most 0.0087.
Values may be sent and summed in bfloat16 or wider, within the bound.
A program may use at most 64 MiB of HBM per device.

v0:
```python
import math
import jax
import jax.numpy as jnp
from jax import lax
from jax.sharding import PartitionSpec as P

HEAD_SIZE = 128
ADAPTER_RANK = 16
NEG_BIG = -1e30
ADAPTER_SCALE = 2.0


def sent_to_all(shard, axis):
    copies = jnp.broadcast_to(shard, (lax.axis_size(axis), *shard.shape))
    return lax.all_to_all(copies, axis, split_axis=0, concat_axis=0, tiled=True)


def over_copies(shard, axis):
    return sent_to_all(shard, axis).sum(axis=0)


def per_device(
    visual_key_value,
    patch_blocks,
    queries,
    suffix_key_value,
    suffix_hidden_state,
    down_weight,
    up_weight,
    question_adapter,
    suffix_token_length,
):
    docs_here, asked_here, suffix_len, query_feature_width = queries.shape
    kv_local = suffix_key_value.shape[3] // (2 * HEAD_SIZE)
    head_group = query_feature_width // (kv_local * HEAD_SIZE)
    asked_rows = asked_here * suffix_len
    row_totals = docs_here * asked_rows
    inverse = 1.0 / math.sqrt(HEAD_SIZE)
    enc_count = lax.axis_size("enc")
    hidden_state_rows = suffix_hidden_state.reshape(row_totals, suffix_hidden_state.shape[3])
    reduced_features = jnp.dot(hidden_state_rows, down_weight, preferred_element_type=jnp.float32)
    owning_question = lax.broadcasted_iota(jnp.int32, (1, down_weight.shape[1]), 1) // ADAPTER_RANK
    row_ids = jnp.broadcast_to(
        question_adapter[:, :, None], (docs_here, asked_here, suffix_len)
    ).reshape(row_totals, 1)
    reduced_features = jnp.where(owning_question == row_ids, reduced_features, 0.0)
    selected_adapter = over_copies(reduced_features, "tp").astype(jnp.bfloat16)
    raised_features = jnp.dot(selected_adapter, up_weight, preferred_element_type=jnp.float32)
    query_matrix = (
        queries.reshape(row_totals, query_feature_width).astype(jnp.float32)
        + ADAPTER_SCALE * raised_features
    ).astype(jnp.bfloat16)
    query_matrix = query_matrix.reshape(docs_here, asked_rows, kv_local, head_group, HEAD_SIZE)
    suffix_pairs = suffix_key_value.reshape(
        docs_here, asked_here, suffix_len, kv_local, 2, HEAD_SIZE
    )
    query_split = query_matrix.reshape(
        docs_here, asked_here, suffix_len, kv_local, head_group, HEAD_SIZE
    )
    suffix_scores = (
        jnp.einsum(
            "bqikgd,bqjkd->bkgqij",
            query_split,
            suffix_pairs[:, :, :, :, 0, :],
            preferred_element_type=jnp.float32,
        )
        * inverse
    )
    positions = lax.broadcasted_iota(jnp.int32, (suffix_len, suffix_len), 0)
    columns = lax.broadcasted_iota(jnp.int32, (suffix_len, suffix_len), 1)
    causal = columns <= positions
    within = (
        lax.broadcasted_iota(jnp.int32, (1, 1, suffix_len), 2) < suffix_token_length[:, :, None]
    )
    suffix_mask = (causal[None, None, :, :] & within[:, :, None, :])[:, None, None]
    suffix_scores = jnp.where(suffix_mask, suffix_scores, NEG_BIG)
    suffix_peak = suffix_scores.max(axis=-1)
    suffix_weights = jnp.where(suffix_mask, jnp.exp(suffix_scores - suffix_peak[..., None]), 0.0)
    running = suffix_peak.reshape(docs_here, kv_local, head_group, asked_rows)
    totals = suffix_weights.sum(axis=-1).reshape(docs_here, kv_local, head_group, asked_rows)
    numerators = jnp.einsum(
        "bkgqij,bqjkd->bkgqid",
        suffix_weights.astype(jnp.bfloat16),
        suffix_pairs[:, :, :, :, 1, :],
        preferred_element_type=jnp.float32,
    )
    numerators = numerators.reshape(docs_here, kv_local, head_group, asked_rows, HEAD_SIZE)
    carried = (running, totals, numerators)
    exchanged = lax.all_to_all(visual_key_value, "enc", split_axis=0, concat_axis=0, tiled=True)
    key_piece = lax.all_gather(exchanged, "seq", axis=1, tiled=True)
    peaks_now, totals_now, numer_now = carried
    tile_rows, page_count, tile_len, piece_width = key_piece.shape
    key_values = key_piece.reshape(enc_count, docs_here, page_count, tile_len, piece_width)
    key_values = jnp.moveaxis(key_values, 1, 0).reshape(
        docs_here, enc_count * page_count * tile_len, kv_local, 2, HEAD_SIZE
    )
    token_pos = lax.broadcasted_iota(
        jnp.int32, (1, enc_count, 1, tile_len), 1
    ) * tile_len + lax.broadcasted_iota(jnp.int32, (1, enc_count, 1, tile_len), 3)
    live_keys = 8 * token_pos < patch_blocks[:, None, :, None] * (enc_count * tile_len)
    live_keys = live_keys.reshape(docs_here, 1, 1, 1, enc_count * page_count * tile_len)
    scores = (
        jnp.einsum(
            "bnkgd,blkd->bkgnl",
            query_matrix,
            key_values[:, :, :, 0, :],
            preferred_element_type=jnp.float32,
        )
        * inverse
    )
    scores = jnp.where(live_keys, scores, NEG_BIG)
    updated = jnp.maximum(peaks_now, scores.max(axis=-1))
    rescale = jnp.exp(peaks_now - updated)
    weights = jnp.where(live_keys, jnp.exp(scores - updated[..., None]), 0.0)
    totals_next = totals_now * rescale + weights.sum(axis=-1)
    numer_next = numer_now * rescale[..., None] + jnp.einsum(
        "bkgnl,blkd->bkgnd",
        weights.astype(jnp.bfloat16),
        key_values[:, :, :, 1, :],
        preferred_element_type=jnp.float32,
    )
    carried = (updated, totals_next, numer_next)
    running, totals, numerators = carried
    context = numerators / totals[..., None]
    context = jnp.transpose(context, (0, 3, 1, 2, 4)).reshape(
        docs_here, asked_here, suffix_len, query_feature_width
    )
    kept_rows = (
        lax.broadcasted_iota(jnp.int32, (1, 1, suffix_len), 2) < suffix_token_length[:, :, None]
    )
    return jnp.where(kept_rows[:, :, :, None], context, 0.0).astype(jnp.bfloat16)


def solution(mesh):
    placed = (
        P(None, "seq", "enc", "tp"),
        P("enc", None),
        P("enc", "seq", None, "tp"),
        P("enc", "seq", None, "tp"),
        P("enc", "seq", None, "tp"),
        P("tp", None),
        P(None, "tp"),
        P("enc", "seq"),
        P("enc", "seq"),
    )
    return jax.shard_map(
        per_device,
        mesh=mesh,
        in_specs=placed,
        out_specs=P("enc", "seq", None, "tp"),
        check_vma=False,
    )
```

profile of v0, /device:TPU:1, one launch (start us, length us, event | category | flops | bytes accessed | tf_op | source)
XLA Modules:
  0.0 128.2 jit_solution(13732557373285925791)
XLA Ops:
  6.5 0.0 copy-start
  6.5 0.0 all-gather.2.cloned.1.call-start
  6.5 45.5 %all_to_all.10 = bf16[16,2,16,512]{3,2,1,0:T(8,128)(2,1)} all-to-all(bf16[16,2,16,512]{3,2,1,0:T(8,128)(2,1)} %param.9), channel_id=1, replica_groups=mesh['enc'=16,'seq'=8,'tp'=4] {'enc'}, dimensions={0} | all-to-all | bytes 1048576 | tf_op jit(solution)/shard_map/all_to_all | solution.py:89
  52.1 0.0 all-gather.2.cloned.1.call-update
  52.1 0.7 broadcast_in_dim.81
  52.8 0.1 broadcast_in_dim.82
  52.9 1.3 %convolution_select_fusion = f32[64,128]{1,0:T(8,128)S(1)} fusion(bf16[64,2048]{1,0:T(8,128)(2,1)} %bitcast.147, bf16[2048,128]{1,0:T(8,128)(2,1)} %param.14, s32[128]{0:T(128)S(1)} %and_select_fusion, s32[64]{0:T(128)S(1)} %broadcast_in_dim.82), kind=kOutput, calls=%fused_computation.24 | convolution fusion | flops 33570816 | bytes 819968 | tf_op jit(solution)/shard_map/dot_general | solution.py:41
  54.3 0.7 broadcast_in_dim.84
  54.9 9.1 %all-to-all-start = ((f32[4,64,128]{2,1,0:T(8,128)}), f32[4,64,128]{2,1,0:T(8,128)S(1)}, u32[]{:S(2)}, u32[]{:S(2)}) async-start(f32[4,64,128]{2,1,0:T(8,128)} %broadcast_in_dim.84), calls=%async_computation | async-start | bytes 262144 | tf_op jit(solution)/shard_map/all_to_all | solution.py:15
  64.0 0.7 multiply_bitcast_fusion
  64.7 0.1 add_multiply_fusion
  64.8 0.1 broadcast_compare_fusion
  64.9 0.1 lt.61
  65.0 0.9 reshape.308
  65.9 0.7 iota_compare_fusion.1
  66.6 0.1 fusion.39
  66.7 2.1 %all-to-all-done = f32[4,64,128]{2,1,0:T(8,128)S(1)} async-done(((f32[4,64,128]{2,1,0:T(8,128)}), f32[4,64,128]{2,1,0:T(8,128)S(1)}, u32[]{:S(2)}, u32[]{:S(2)}) %all-to-all-start) | async-done | bytes 131104 | tf_op jit(solution)/shard_map/all_to_all | solution.py:15
  68.8 0.0 copy-done
  68.8 1.2 fusion.17
  70.1 0.4 fusion.40
  70.4 0.4 fusion.25
  70.8 0.2 convolution_bitcast_fusion
  71.1 19.3 %all-gather.2.cloned.1.call-done = bf16[16,16,16,512]{3,2,1,0:T(8,128)(2,1)} async-done(((bf16[16,2,16,512]{3,2,1,0:T(8,128)(2,1)}), bf16[16,16,16,512]{3,2,1,0:T(8,128)(2,1)}) %all-gather.2.cloned.1.call-update) | async-done | bytes 4194320 | tf_op jit(solution)/shard_map/all_gather | solution.py:90
  90.3 6.9 %reshape_transpose_reshape.3 = bf16[1,4096,2,2,128]{4,3,2,1,0:T(2,128)(2,1)} reshape(bf16[16,16,16,512]{3,2,1,0:T(8,128)(2,1)} %all-gather.2.cloned.1.call-done) | data formatting | bytes 8388608 | tf_op jit(solution)/shard_map/reshape;transpose;reshape | solution.py:94
  97.2 9.0 %fusion.38 = (bf16[1,4096,2,1,128]{4,3,2,1,0:T(2,128)(2,1)S(1)}, bf16[1,4096,2,1,128]{4,3,2,1,0:T(2,128)(2,1)S(1)}) fusion(bf16[1,4096,2,2,128]{4,3,2,1,0:T(2,128)(2,1)} %reshape_transpose_reshape.3), kind=kLoop, calls=%fused_computation.56 | loop fusion | bytes 8388608 | tf_op jit(solution)/shard_map/slice | solution.py:106
  106.2 2.9 %fusion.1 = (f32[2,8,64]{1,2,0:T(8,128)S(1)}, f32[2,64,8,4096]{3,2,1,0:T(8,128)S(1)}) fusion(pred[4096]{0:T(1024)(128)(4,1)S(1)} %lt.61, bf16[1,4096,2,1,128]{4,3,2,1,0:T(2,128)(2,1)S(1)} %get-tuple-element.7, bf16[64,2,8,128]{3,2,1,0:T(8,128)(2,1)S(1)} %bitcast.143), kind=kOutput, calls=%fused_computation.3 | convolution fusion | flops 1086323712 | bytes 19144704 | tf_op jit(solution)/shard_map/bnkgd,blkd->bkgnl/dot_general | solution.py:103
  109.2 4.9 %fusion.2 = f32[2,8,64]{1,2,0:T(8,128)S(1)} fusion(f32[2,64,8,4096]{3,2,1,0:T(8,128)S(1)} %get-tuple-element.16, f32[2,8,64]{1,2,0:T(8,128)S(1)} %max.17, pred[4096]{0:T(1024)(128)(4,1)S(1)} %lt.61), kind=kLoop, calls=%fused_computation.4 | loop fusion | flops 20970496 | bytes 16789504 | tf_op jit(solution)/shard_map/reduce_sum | solution.py:115
  114.1 4.8 %fusion.21 = f32[1,64,2,8,128]{4,3,1,2,0:T(8,128)} fusion(bf16[1,4096,2,1,128]{4,3,2,1,0:T(2,128)(2,1)S(1)} %get-tuple-element.8, f32[2,64,8,4096]{3,2,1,0:T(8,128)S(1)} %get-tuple-element.16, f32[2,8,64]{1,2,0:T(8,128)S(1)} %max.17, pred[4096]{0:T(1024)(128)(4,1)S(1)} %lt.61, f32[2,8,64,128]{3,2,1,0:T(8,128)S(1)} %bitcast.146, ...), kind=kOutput, calls=%fused_computation.23 | convolution fusion | flops 1095106560 | bytes 19939328 | tf_op jit(solution)/shard_map/bkgnl,blkd->bkgnd/dot_general | solution.py:116
  118.9 1.1 copy.38
  120.0 0.5 fusion.24
  120.5 0.9 copy.39
  (9 shorter events, 0.1 us)
Async XLA Ops:
  6.5 62.3 %copy-start = (bf16[128,2048]{1,0:T(8,128)(2,1)S(1)}, bf16[128,2048]{1,0:T(8,128)(2,1)}, u32[]{:S(2)}) copy-start(bf16[128,2048]{1,0:T(8,128)(2,1)} %param.15) | copy-start | bytes 1572868
  6.5 83.8 %all-gather.2.cloned.1.call-start = ((), (), s32[]{:S(2)}) async-start(), calls=%async_computation.2 | async-start | bytes 4718592 | tf_op jit(solution)/shard_map/all_gather | solution.py:90
  54.9 13.9 %all-to-all-start = ((f32[4,64,128]{2,1,0:T(8,128)}), f32[4,64,128]{2,1,0:T(8,128)S(1)}, u32[]{:S(2)}, u32[]{:S(2)}) async-start(f32[4,64,128]{2,1,0:T(8,128)} %broadcast_in_dim.84), calls=%async_computation | async-start | bytes 262144 | tf_op jit(solution)/shard_map/all_to_all | solution.py:15
Sparse Core Ops, SparseCore 0:
  52.2 38.0 all-gather.1
where the time goes:
time: 129 us; the launch traced here: 128 us
  blocking collectives  45.5 us (35%)
  waiting for transfers between devices  21.4 us (17%)
  local copies, waits for them, and re-layouts  20.4 us (16%)
  between operations  13.5 us (10%)
  matrix products  10.8 us (8%)
  starting transfers between devices  9.1 us (7%)
  other arithmetic  7.44 us (6%)
    all_to_all x1, blocking collectives, per_device(): lax.all_to_all(visual_key_value, 'enc', split_axis=0, concat_axis=0, tile...  45.5 us
    all_gather x1, waiting for transfers between devices, per_device(): key_piece = lax.all_gather(exchanged, 'seq', axis=1, tiled=True)  19.3 us
    all_to_all x1, starting transfers between devices, sent_to_all(): return lax.all_to_all(copies, axis, split_axis=0, concat_axis=0, tiled=True)  9.1 us
    slice x1, local copies, waits for them, and re-layouts, per_device(): key_values[:, :, :, 0, :]  8.97 us
    another operation x1, local copies, waits for them, and re-layouts, per_device(): jnp.moveaxis(key_values, 1, 0)  6.92 us
    reduce_sum x1, other arithmetic, per_device(): totals_next = totals_now * rescale + weights.sum(axis=-1)  4.91 us
    dot_general x1, matrix products, per_device(): jnp.einsum('bkgnl,blkd->bkgnd', weights.astype(jnp.bfloat16), key_values[...  4.77 us
    dot_general x1, matrix products, per_device(): jnp.einsum('bnkgd,blkd->bkgnl', query_matrix, key_values[:, :, :, 0, :],...  2.92 us
  transfers between devices with their start and end apart: 2, of which 2 were waited for; matrix products, arithmetic and copies ran while one was open for 6% of the time, Pallas kernels for 0%

commit v1 on v0

--- a/solution.py
+++ b/solution.py
@@ -87,7 +87,9 @@
     numerators = numerators.reshape(docs_here, kv_local, head_group, asked_rows, HEAD_SIZE)
     carried = (running, totals, numerators)
     exchanged = lax.all_to_all(visual_key_value, "enc", split_axis=0, concat_axis=0, tiled=True)
-    key_piece = lax.all_gather(exchanged, "seq", axis=1, tiled=True)
+    key_piece = jnp.concatenate(
+        lax.all_to_all(jnp.stack([exchanged] * lax.axis_size("seq")), "seq", 0, 0), axis=1
+    )
     peaks_now, totals_now, numer_now = carried
     tile_rows, page_count, tile_len, piece_width = key_piece.shape
     key_values = key_piece.reshape(enc_count, docs_here, page_count, tile_len, piece_width)

time: 129 us -> 155 us (1.20)
  the two profiles are of different devices: /device:TPU:1 before, /device:TPU:32 now
where the time goes in v1:
time: 155 us; the launch traced here: 154 us
  blocking collectives  59.3 us (38%)
  waiting for transfers between devices  44.8 us (29%)
  local copies, waits for them, and re-layouts  27.3 us (18%)
  matrix products  10.8 us (7%)
  other arithmetic  7.44 us (5%)
  starting transfers between devices  4.54 us (3%)
    all_to_all x1, blocking collectives, per_device(): lax.all_to_all(visual_key_value, 'enc', split_axis=0, concat_axis=0, tile...  46.2 us
    all_to_all x1, waiting for transfers between devices, per_device(): lax.all_to_all(jnp.stack([exchanged] * lax.axis_size('seq')), 'seq', 0, 0)  44.8 us
    all_to_all x1, blocking collectives, sent_to_all(): return lax.all_to_all(copies, axis, split_axis=0, concat_axis=0, tiled=True)  13 us
    slice x1, local copies, waits for them, and re-layouts, per_device(): key_values[:, :, :, 0, :]  8.9 us
    another operation x1, local copies, waits for them, and re-layouts, per_device(): jnp.moveaxis(key_values, 1, 0)  6.93 us
    reshape x1, local copies, waits for them, and re-layouts, per_device(): jnp.concatenate(lax.all_to_all(jnp.stack([exchanged] * lax.axis_size('seq...  5 us
    reduce_sum x1, other arithmetic, per_device(): totals_next = totals_now * rescale + weights.sum(axis=-1)  4.91 us
    dot_general x1, matrix products, per_device(): jnp.einsum('bkgnl,blkd->bkgnd', weights.astype(jnp.bfloat16), key_values[...  4.77 us
  transfers between devices with their start and end apart: 1, of which 1 were waited for; matrix products, arithmetic and copies ran while one was open for 3% of the time, Pallas kernels for 0%

profile of v1, /device:TPU:32, one launch (start us, length us, event | category | flops | bytes accessed | tf_op | source)
XLA Modules:
  0.0 154.2 jit_solution(2684932294754566327)
XLA Ops:
  0.0 0.0 copy-start
  0.0 0.8 broadcast_in_dim.81
  0.8 0.1 broadcast_in_dim.82
  0.9 1.3 convolution_select_fusion
  2.2 13.0 %all_to_all.15 = f32[4,64,128]{2,1,0:T(8,128)S(1)} all-to-all(f32[4,64,128]{2,1,0:T(8,128)S(1)} %broadcast_in_dim.84), channel_id=1, replica_groups=mesh['enc'=16,'seq'=8,'tp'=4] {'tp'}, dimensions={0} | all-to-all | bytes 262144 | tf_op jit(solution)/shard_map/all_to_all | solution.py:15
  15.3 46.2 %all_to_all.16 = bf16[16,2,16,512]{3,2,1,0:T(8,128)(2,1)S(1)} all-to-all(bf16[16,2,16,512]{3,2,1,0:T(8,128)(2,1)} %param.9), channel_id=1, replica_groups=mesh['enc'=16,'seq'=8,'tp'=4] {'enc'}, dimensions={0} | all-to-all | bytes 1048576 | tf_op jit(solution)/shard_map/all_to_all | solution.py:89
  61.5 2.5 %stack.2 = bf16[8,16,2,16,512]{4,3,2,1,0:T(8,128)(2,1)} broadcast(bf16[16,2,16,512]{3,2,1,0:T(8,128)(2,1)S(1)} %all_to_all.16), dimensions={1,2,3,4} | broadcast | bytes 4718592 | tf_op jit(solution)/shard_map/stack | solution.py:91
  64.0 4.5 %all-to-all-start.2 = ((bf16[8,16,2,16,512]{4,3,2,1,0:T(8,128)(2,1)}), bf16[8,16,2,16,512]{4,3,2,1,0:T(8,128)(2,1)}, u32[]{:S(2)}, u32[]{:S(2)}) async-start(bf16[8,16,2,16,512]{4,3,2,1,0:T(8,128)(2,1)} %stack.2), calls=%async_computation.2 | async-start | bytes 8388608 | tf_op jit(solution)/shard_map/all_to_all | solution.py:91
  68.6 0.7 multiply_bitcast_fusion
  69.2 0.1 add_multiply_fusion
  69.3 0.1 broadcast_compare_fusion
  69.4 0.1 lt.61
  69.5 0.9 reshape.313
  70.4 0.7 iota_compare_fusion.1
  71.1 0.1 fusion.39
  71.3 0.0 copy-done
  71.3 1.2 fusion.17
  72.5 0.4 fusion.40
  72.9 0.4 fusion.25
  73.3 0.2 convolution_bitcast_fusion
  73.5 44.8 %all-to-all-done.2 = bf16[8,16,2,16,512]{4,3,2,1,0:T(8,128)(2,1)} async-done(((bf16[8,16,2,16,512]{4,3,2,1,0:T(8,128)(2,1)}), bf16[8,16,2,16,512]{4,3,2,1,0:T(8,128)(2,1)}, u32[]{:S(2)}, u32[]{:S(2)}) %all-to-all-start.2) | async-done | bytes 4194336 | tf_op jit(solution)/shard_map/all_to_all | solution.py:91
  118.3 5.0 %copy.46 = bf16[16,8,2,16,512]{4,3,2,1,0:T(8,128)(2,1)} copy(bf16[16,8,2,16,512]{4,3,2,0,1:T(8,128)(2,1)} %bitcast.20) | data formatting | bytes 8388608 | tf_op jit(solution)/shard_map/reshape | solution.py:90
  123.3 6.9 %reshape_transpose_reshape_reshape.3 = bf16[1,4096,2,2,128]{4,3,2,1,0:T(2,128)(2,1)} reshape(bf16[16,8,2,16,512]{4,3,2,1,0:T(8,128)(2,1)} %copy.46) | data formatting | bytes 8388608 | tf_op jit(solution)/shard_map/reshape;transpose;reshape;reshape | solution.py:96
  130.2 8.9 %fusion.38 = (bf16[1,4096,2,1,128]{4,3,2,1,0:T(2,128)(2,1)S(1)}, bf16[1,4096,2,1,128]{4,3,2,1,0:T(2,128)(2,1)S(1)}) fusion(bf16[1,4096,2,2,128]{4,3,2,1,0:T(2,128)(2,1)} %reshape_transpose_reshape_reshape.3), kind=kLoop, calls=%fused_computation.56 | loop fusion | bytes 8388608 | tf_op jit(solution)/shard_map/slice | solution.py:108
  139.1 2.9 %fusion.1 = (f32[2,8,64]{1,2,0:T(8,128)S(1)}, f32[2,64,8,4096]{3,2,1,0:T(8,128)S(1)}) fusion(pred[4096]{0:T(1024)(128)(4,1)S(1)} %lt.61, bf16[1,4096,2,1,128]{4,3,2,1,0:T(2,128)(2,1)S(1)} %get-tuple-element.7, bf16[64,2,8,128]{3,2,1,0:T(8,128)(2,1)S(1)} %bitcast.144), kind=kOutput, calls=%fused_computation.3 | convolution fusion | flops 1086323712 | bytes 19144704 | tf_op jit(solution)/shard_map/bnkgd,blkd->bkgnl/dot_general | solution.py:105
  142.0 4.9 %fusion.2 = f32[2,8,64]{1,2,0:T(8,128)S(1)} fusion(f32[2,64,8,4096]{3,2,1,0:T(8,128)S(1)} %get-tuple-element.16, f32[2,8,64]{1,2,0:T(8,128)S(1)} %max.17, pred[4096]{0:T(1024)(128)(4,1)S(1)} %lt.61), kind=kLoop, calls=%fused_computation.4 | loop fusion | flops 20970496 | bytes 16789504 | tf_op jit(solution)/shard_map/reduce_sum | solution.py:117
  147.0 4.8 %fusion.21 = f32[1,64,2,8,128]{4,3,1,2,0:T(8,128)} fusion(bf16[1,4096,2,1,128]{4,3,2,1,0:T(2,128)(2,1)S(1)} %get-tuple-element.8, f32[2,64,8,4096]{3,2,1,0:T(8,128)S(1)} %get-tuple-element.16, f32[2,8,64]{1,2,0:T(8,128)S(1)} %max.17, pred[4096]{0:T(1024)(128)(4,1)S(1)} %lt.61, f32[2,8,64,128]{3,2,1,0:T(8,128)S(1)} %bitcast.147, ...), kind=kOutput, calls=%fused_computation.23 | convolution fusion | flops 1095106560 | bytes 19939328 | tf_op jit(solution)/shard_map/bkgnl,blkd->bkgnd/dot_general | solution.py:118
  151.7 1.1 copy.51
  152.8 0.5 fusion.24
  153.4 0.9 copy.52
  (10 shorter events, 0.2 us)
Async XLA Ops:
  0.0 71.3 %copy-start = (bf16[128,2048]{1,0:T(8,128)(2,1)S(1)}, bf16[128,2048]{1,0:T(8,128)(2,1)}, u32[]{:S(2)}) copy-start(bf16[128,2048]{1,0:T(8,128)(2,1)} %param.15) | copy-start | bytes 1572868
  64.0 54.3 %all-to-all-start.2 = ((bf16[8,16,2,16,512]{4,3,2,1,0:T(8,128)(2,1)}), bf16[8,16,2,16,512]{4,3,2,1,0:T(8,128)(2,1)}, u32[]{:S(2)}, u32[]{:S(2)}) async-start(bf16[8,16,2,16,512]{4,3,2,1,0:T(8,128)(2,1)} %stack.2), calls=%async_computation.2 | async-start | bytes 8388608 | tf_op jit(solution)/shard_map/all_to_all | solution.py:91
